TPU v7x, 32 devices: a whole 2x2x4 slice. The times are simulated.
32 devices in a mesh: leaf: 8 (over z, y), rhs: 4 (over x, core).
Axes of the slice: x: 2, y: 2, z: 4, core: 2. Of those that a mesh axis runs over, the one named last changes fastest.
Arguments:
- densities: bfloat16 [64, 32768], P('rhs', 'leaf'), may hold values from -6 to 6
- bases: float32 [32, 32768], P(None, 'leaf'), may hold values from -0.5 to 0.5
- near_blocks: bfloat16 [256, 8, 128, 128], P('leaf', 'rhs'), may hold values from -0.1875 to 0.1875
- near_src: int32 [256, 8], P('leaf', 'rhs'), may hold values from 0 to 55, as said below
- send_leaf: int32 [8, 6, 4], replicated, may hold values from -1 to 31, as said below
- far_src: int32 [256, 8], P('leaf'), may hold values from 0 to 31
- leaf_coupling: float32 [256, 8, 32, 32], P('leaf'), may hold values from -0.375 to 0.375
- local_transfer: float32 [8, 64, 32, 32], P('leaf'), may hold values from -0.75 to 0.75
- upper_transfer: float32 [16, 32, 32], replicated, may hold values from -0.75 to 0.75
- up_coupling: float32 [16, 3, 32, 32], replicated, may hold values from -8 to 8
Outputs:
- product: float32 [64, 32768], P('rhs', 'leaf')
Inputs may be any that keep to these rules, and one draw needn't show every extreme that they name: `send_leaf`: entry [e, j, c] is a leaf of device e (local index) whose panel e sends to its face neighbour e + o_j, or -1. Only existing face neighbours receive; the leaves of [e, j] are distinct and come before the -1 entries; every device sends exactly 4 leaves to at least one neighbour, among them its leaf 32 - 1, and exactly 4 to its neighbour at offset -s*s where that exists. `near_src`: A slot of the owner's panel buffer: below 32 a leaf of the same device, else slot 32 + j * 4 + c. It never names an empty slot, and every filled slot is named by some block of the device.
All inputs are finite; a program needn't handle non-finite values.
Results may differ from a plain program's by a relative error of at most 0.0003.
Values may be sent and summed in bfloat16 or wider, within the bound.
No kernel may reach another device: no remote copies, remote signals or barrier semaphores. Data moves between devices by JAX's collectives and lax.ppermute only.
A program may use at most 128 MiB of HBM per device.

v0:
```python
import jax
import jax.numpy as jnp
from jax import lax
from jax.sharding import PartitionSpec as P

TOP_PREC = lax.Precision.HIGHEST
FACE_SIGNS = ((1, 0), (-1, 0), (1, 1), (-1, 1), (1, 2), (-1, 2))


def shifted(value, axis, steps):
    count = lax.axis_size(axis)
    first, last = (max(0, -steps), min(count, count - steps))
    return lax.ppermute(value, axis, [(source, source + steps) for source in range(first, last)])


def cube_side(device_count):
    return max((edge_len for edge_len in range(1, 65) if edge_len**3 <= device_count))


def face_offsets(device_count):
    side_len = cube_side(device_count)
    return [face_sign * side_len**axis_pos for face_sign, axis_pos in FACE_SIGNS]


def lift_pairs(child_coef, child_maps):
    lifted = jnp.einsum("...nrs,...nqr->...nqs", child_maps, child_coef, precision=TOP_PREC)
    return lifted[..., 0::2, :, :] + lifted[..., 1::2, :, :]


def apply_maps(node_maps, coef_rows):
    return jnp.einsum("...nrs,...nqs->...nqr", node_maps, coef_rows, precision=TOP_PREC)


def couple_level(coef_level, maps_level):
    level_width = coef_level.shape[0]
    even_node = jnp.arange(level_width) % 2 == 0
    padded = jnp.pad(coef_level, ((3, 3), (0, 0), (0, 0)))
    minus_two = padded[1 : level_width + 1]
    plus_two = padded[5 : level_width + 5]
    third_node = jnp.where(
        even_node[:, None, None], padded[6 : level_width + 6], padded[0:level_width]
    )
    first_terms = apply_maps(maps_level[:, 0], minus_two) + apply_maps(maps_level[:, 1], plus_two)
    return first_terms + apply_maps(maps_level[:, 2], third_node)


def upper_tree(roots, upper_transfer, up_coupling):
    node_total = roots.shape[0]
    coef_levels = {node_total: roots}
    level_width = node_total
    while level_width > 4:
        coef_levels[level_width // 2] = lift_pairs(
            coef_levels[level_width], upper_transfer[level_width : 2 * level_width]
        )
        level_width = level_width // 2
    level_field = couple_level(coef_levels[4], up_coupling[4:8])
    level_width = 4
    while level_width < node_total:
        level_width = level_width * 2
        coupled = couple_level(coef_levels[level_width], up_coupling[level_width : 2 * level_width])
        level_field = coupled + apply_maps(
            upper_transfer[level_width : 2 * level_width], jnp.repeat(level_field, 2, axis=0)
        )
    return level_field


def local(
    densities,
    bases,
    near_blocks,
    near_src,
    send_leaf,
    far_src,
    leaf_coupling,
    local_transfer,
    upper_transfer,
    up_coupling,
):
    leaf_devices = lax.axis_size("leaf")
    device_rank = lax.axis_index("leaf")
    columns, points = densities.shape
    leaf_count = near_blocks.shape[0]
    leaf_width = near_blocks.shape[2]
    rank_width = bases.shape[0]
    panels = densities.reshape(columns, leaf_count, leaf_width)
    offsets = face_offsets(leaf_devices)
    arrived = []
    for direction in range(6):
        neighbour_panels = shifted(panels, "leaf", offsets[direction])
        sender = device_rank - offsets[direction]
        inside = (sender >= 0) & (sender < leaf_devices)
        clipped = jnp.clip(sender, 0, leaf_devices - 1)
        sent_leaf = lax.dynamic_index_in_dim(send_leaf, clipped, 0, keepdims=False)[direction]
        chosen = jnp.take(neighbour_panels, jnp.maximum(sent_leaf, 0), axis=1)
        keep_slot = inside & (sent_leaf >= 0)
        arrived.append(jnp.where(keep_slot[None, :, None], chosen, jnp.zeros_like(chosen)))
    buffer = jnp.concatenate([panels] + arrived, axis=1)
    piece_blocks = lax.all_gather(near_blocks, "rhs", axis=1, tiled=True)
    piece_sources = lax.all_gather(near_src, "rhs", axis=1, tiled=True)
    picked = jnp.take(buffer, piece_sources, axis=1)
    near_field = jnp.einsum(
        "tkij,qtkj->qti", piece_blocks, picked, preferred_element_type=jnp.float32
    )
    near_field = near_field.reshape(columns, points)
    basis_view = bases.reshape(rank_width, leaf_count, leaf_width)
    leaf_coef = jnp.einsum(
        "rti,qti->tqr", basis_view, panels.astype(jnp.float32), precision=TOP_PREC
    )
    subtree_maps = local_transfer[0]
    coef_levels = {leaf_count: leaf_coef}
    level_width = leaf_count
    while level_width > 1:
        coef_levels[level_width // 2] = lift_pairs(
            coef_levels[level_width], subtree_maps[level_width : 2 * level_width]
        )
        level_width = level_width // 2
    root_coef = coef_levels[1][0]
    roots = lax.all_gather(root_coef[None], "leaf", axis=0, tiled=True)
    root_all = upper_tree(roots, upper_transfer, up_coupling)
    root_field = lax.dynamic_index_in_dim(root_all, device_rank, 0, keepdims=False)
    picked_coef = jnp.take(leaf_coef, far_src, axis=0)
    leaf_local = jnp.einsum("tjrs,tjqs->tqr", leaf_coupling, picked_coef, precision=TOP_PREC)
    level_field = root_field[None]
    level_width = 1
    while level_width < leaf_count:
        level_width = level_width * 2
        level_field = apply_maps(
            subtree_maps[level_width : 2 * level_width], jnp.repeat(level_field, 2, axis=0)
        )
    leaf_field = level_field + leaf_local
    far_part = jnp.einsum("rti,tqr->qti", basis_view, leaf_field, precision=TOP_PREC).reshape(
        columns, points
    )
    return near_field + far_part


def solution(mesh):
    in_specs = (
        P("rhs", "leaf"),
        P(None, "leaf"),
        P("leaf", "rhs", None, None),
        P("leaf", "rhs"),
        P(),
        P("leaf", None),
        P("leaf", None, None, None),
        P("leaf", None, None, None),
        P(),
        P(),
    )
    out_specs = P("rhs", "leaf")
    return jax.shard_map(local, mesh=mesh, in_specs=in_specs, out_specs=out_specs, check_vma=False)
```

profile of v0, /device:TPU:0, one launch (start us, length us, event | category | flops | bytes accessed | tf_op | source)
XLA Modules:
  0.0 119.4 jit_solution(8004651650733961316)
XLA Ops:
  6.5 0.7 all-gather.3.cloned.1.call-update
  8.2 5.5 %collective-permute-start = (bf16[16,32,128]{2,0,1:T(8,128)(2,1)}, bf16[16,32,128]{2,0,1:T(8,128)(2,1)}, u32[]{:S(2)}, u32[]{:S(2)}) collective-permute-start(bf16[16,32,128]{2,0,1:T(8,128)(2,1)} %copy_bitcast_fusion.1), channel_id=1, source_target_pairs={{0,4},{4,8},{8,12},{12,16},{16,20},{20,24},{24,28},{1,5},{5,9},{9,... | collective-permute-start | bytes 393224 | tf_op jit(solution)/shard_map/ppermute | solution.py:13
  13.7 1.3 %collective-permute-start.1 = (bf16[16,32,128]{2,0,1:T(8,128)(2,1)}, bf16[16,32,128]{2,0,1:T(8,128)(2,1)}, u32[]{:S(2)}, u32[]{:S(2)}) collective-permute-start(bf16[16,32,128]{2,0,1:T(8,128)(2,1)} %copy_bitcast_fusion.1), channel_id=1, source_target_pairs={{4,0},{8,4},{12,8},{16,12},{20,16},{24,20},{28,24},{5,1},{9,5},{13... | collective-permute-start | bytes 393224 | tf_op jit(solution)/shard_map/ppermute | solution.py:13
  15.0 5.5 %collective-permute-start.2 = (bf16[16,32,128]{2,0,1:T(8,128)(2,1)}, bf16[16,32,128]{2,0,1:T(8,128)(2,1)}, u32[]{:S(2)}, u32[]{:S(2)}) collective-permute-start(bf16[16,32,128]{2,0,1:T(8,128)(2,1)} %copy_bitcast_fusion.1), channel_id=1, source_target_pairs={{0,8},{4,12},{8,16},{12,20},{16,24},{20,28},{1,9},{5,13},{9,17},{1... | collective-permute-start | bytes 393224 | tf_op jit(solution)/shard_map/ppermute | solution.py:13
  20.5 1.3 %collective-permute-start.3 = (bf16[16,32,128]{2,0,1:T(8,128)(2,1)}, bf16[16,32,128]{2,0,1:T(8,128)(2,1)}, u32[]{:S(2)}, u32[]{:S(2)}) collective-permute-start(bf16[16,32,128]{2,0,1:T(8,128)(2,1)} %copy_bitcast_fusion.1), channel_id=1, source_target_pairs={{8,0},{12,4},{16,8},{20,12},{24,16},{28,20},{9,1},{13,5},{17,9},{2... | collective-permute-start | bytes 393224 | tf_op jit(solution)/shard_map/ppermute | solution.py:13
  21.8 5.6 %collective-permute-start.4 = (bf16[16,32,128]{2,0,1:T(8,128)(2,1)}, bf16[16,32,128]{2,0,1:T(8,128)(2,1)}, u32[]{:S(2)}, u32[]{:S(2)}) collective-permute-start(bf16[16,32,128]{2,0,1:T(8,128)(2,1)} %copy_bitcast_fusion.1), channel_id=1, source_target_pairs={{0,16},{4,20},{8,24},{12,28},{1,17},{5,21},{9,25},{13,29},{2,18},{... | collective-permute-start | bytes 393224 | tf_op jit(solution)/shard_map/ppermute | solution.py:13
  27.4 1.1 slice.157
  28.5 1.0 slice.161
  30.2 1.5 %copy.100 = f32[1,32,32,32]{3,2,1,0:T(8,128)S(1)} copy(f32[1,32,32,32]{1,3,2,0:T(8,128)} %slice.157) | data formatting | bytes 262144
  31.7 2.0 %copy.101 = f32[1,16,32,32]{3,2,1,0:T(8,128)} copy(f32[1,16,32,32]{1,3,2,0:T(8,128)} %slice.161) | data formatting | bytes 131072
  33.7 0.9 copy.102
  34.5 0.9 copy.103
  35.4 0.9 copy.104
  36.3 5.1 %all-gather = s32[4,2,32]{2,1,0:T(2,128)S(1)} all-gather(s32[1,2,32]{2,1,0:T(2,128)S(1)} %bitcast.157), channel_id=1, replica_groups=mesh['leaf'=8,'rhs'=4] {'rhs'}, dimensions={0}, use_global_device_ids=true | all-gather | bytes 1280 | tf_op jit(solution)/shard_map/all_gather | solution.py:99
  42.2 0.7 copy.94
  43.4 1.0 gather_fusion.1
  45.3 1.4 %fusion.23 = f32[16,16,32]{2,1,0:T(8,128)S(1)} fusion(f32[1,16,32,32]{3,2,1,0:T(8,128)} %copy.101, f32[32,16,32]{2,1,0:T(8,128)S(1)} %fusion.16), kind=kOutput, calls=%fused_computation.34 | convolution fusion | flops 3153920 | bytes 163840 | tf_op jit(solution)/shard_map/...nrs,...nqr->...nqs/dot_general | solution.py:26
  46.7 1.3 %fusion.33 = f32[8,16,32]{2,1,0:T(8,128)S(1)} fusion(f32[1,8,32,32]{3,2,1,0:T(8,128)} %copy.102, f32[16,16,32]{2,1,0:T(8,128)S(1)} %fusion.23), kind=kOutput, calls=%fused_computation.47 | convolution fusion | flops 1576960 | bytes 81920 | tf_op jit(solution)/shard_map/...nrs,...nqr->...nqs/dot_general | solution.py:26
  48.0 1.0 fusion.54
  49.1 0.9 fusion.66
  50.0 30.5 %all_gather.11 = f32[8,16,32]{2,1,0:T(8,128)S(1)} all-gather(f32[1,16,32]{2,1,0:T(8,128)S(1)} %slice_add_fusion.1), channel_id=1, replica_groups=mesh['leaf'=8,'rhs'=4] {'leaf'}, dimensions={0}, use_global_device_ids=true | all-gather | bytes 18432 | tf_op jit(solution)/shard_map/all_gather | solution.py:118
  90.0 3.8 %fusion.2 = f32[32,16,32]{2,1,0:T(8,128)S(1)} fusion(f32[32,8,32,32]{3,2,1,0:T(8,128)S(1)} %copy-done.2, f32[32,8,16,32]{3,2,1,0:T(8,128)S(1)} %bitcast.148, pred[32,8]{1,0:T(8,128)(4,1)S(1)} %copy-done.15), kind=kOutput, calls=%fused_computation.10 | convolution fusion | flops 50462720 | bytes 1638656 | tf_op jit(solution)/shard_map/tjrs,tjqs->tqr/dot_general | solution.py:122
  93.9 0.9 convolution_add_fusion.1
  94.8 1.3 %collective-permute-start.5 = (bf16[16,32,128]{2,0,1:T(8,128)(2,1)}, bf16[16,32,128]{2,0,1:T(8,128)(2,1)S(1)}, u32[]{:S(2)}, u32[]{:S(2)}) collective-permute-start(bf16[16,32,128]{2,0,1:T(8,128)(2,1)} %copy_bitcast_fusion.1), channel_id=1, source_target_pairs={{16,0},{20,4},{24,8},{28,12},{17,1},{21,5},{25,9},{29,13},{18,2},{... | collective-permute-start | bytes 393224 | tf_op jit(solution)/shard_map/ppermute | solution.py:13
  96.7 1.6 %gather_fusion.2 = bf16[4,16,128]{2,1,0:T(8,128)(2,1)S(1)} fusion(bf16[16,32,128]{2,0,1:T(8,128)(2,1)} %collective-permute-done, s32[1024]{0:T(1024)} %pad_clamp_fusion.7), kind=kCustom, calls=%fused_computation.clone | custom fusion | bytes 32784 | tf_op jit(solution)/shard_map/jit(_take)/gather | solution.py:94
  98.3 1.6 %gather_fusion.3 = bf16[4,16,128]{2,1,0:T(8,128)(2,1)S(1)} fusion(bf16[16,32,128]{2,0,1:T(8,128)(2,1)} %collective-permute-done.1, s32[1024]{0:T(1024)} %pad_clamp_fusion.6), kind=kCustom, calls=%fused_computation.1.clone | custom fusion | bytes 32784 | tf_op jit(solution)/shard_map/jit(_take)/gather | solution.py:94
  99.9 1.6 %gather_fusion.4 = bf16[4,16,128]{2,1,0:T(8,128)(2,1)S(1)} fusion(bf16[16,32,128]{2,0,1:T(8,128)(2,1)} %collective-permute-done.2, s32[1024]{0:T(1024)} %pad_clamp_fusion.5), kind=kCustom, calls=%fused_computation.2.clone | custom fusion | bytes 32784 | tf_op jit(solution)/shard_map/jit(_take)/gather | solution.py:94
  101.5 1.5 %gather_fusion.5 = bf16[4,16,128]{2,1,0:T(8,128)(2,1)S(1)} fusion(bf16[16,32,128]{2,0,1:T(8,128)(2,1)} %collective-permute-done.3, s32[1024]{0:T(1024)S(1)} %pad_clamp_fusion.4), kind=kCustom, calls=%fused_computation.3.clone | custom fusion | bytes 32784 | tf_op jit(solution)/shard_map/jit(_take)/gather | solution.py:94
  103.0 1.5 %gather_fusion.6 = bf16[4,16,128]{2,1,0:T(8,128)(2,1)S(1)} fusion(bf16[16,32,128]{2,0,1:T(8,128)(2,1)} %collective-permute-done.4, s32[1024]{0:T(1024)S(1)} %pad_clamp_fusion.3), kind=kCustom, calls=%fused_computation.4.clone | custom fusion | bytes 32784 | tf_op jit(solution)/shard_map/jit(_take)/gather | solution.py:94
  105.6 0.8 gather_fusion
  106.5 4.7 %convolution_bitcast_fusion = f32[32,16,128]{2,1,0:T(8,128)S(1)} fusion(bf16[32,8,128,128]{3,2,1,0:T(8,128)(2,1)} %all-gather.3.cloned.1.call-done, bf16[32,8,16,128]{3,2,1,0:T(8,128)(2,1)S(1)} %bitcast.149, pred[32,8]{1,0:T(8,128)(4,1)S(1)} %copy.72), kind=kOutput, calls=%fused_computation.14 | convolution fusion | flops 134742016 | bytes 9699584 | tf_op jit(solution)/shard_map/tkij,qtkj->qti/dot_general | solution.py:101
  111.8 0.7 copy.127
  (123 shorter events, 15.3 us)
Async XLA Ops:
  6.5 36.3 %copy-start = (f32[32,4096]{1,0:T(8,128)S(1)}, f32[32,4096]{1,0:T(8,128)}, u32[]{:S(2)}) copy-start(f32[32,4096]{1,0:T(8,128)} %param.13) | copy-start | bytes 1572868
  6.5 1.0 copy-start.4
  6.5 20.8 %copy-start.1 = (f32[1,64,32,32]{1,3,2,0:T(8,128)S(1)}, f32[1,64,32,32]{1,3,2,0:T(8,128)}, u32[]{:S(2)}) copy-start(f32[1,64,32,32]{1,3,2,0:T(8,128)} %param.19) | copy-start | bytes 786436
  6.5 100.0 %all-gather.3.cloned.1.call-start = ((), (), s32[]{:S(2)}) async-start(), calls=%async_computation | async-start | bytes 10485760 | tf_op jit(solution)/shard_map/all_gather | solution.py:98
  8.2 86.6 %collective-permute-start = (bf16[16,32,128]{2,0,1:T(8,128)(2,1)}, bf16[16,32,128]{2,0,1:T(8,128)(2,1)}, u32[]{:S(2)}, u32[]{:S(2)}) collective-permute-start(bf16[16,32,128]{2,0,1:T(8,128)(2,1)} %copy_bitcast_fusion.1), channel_id=1, source_target_pairs={{0,4},{4,8},{8,12},{12,16},{16,20},{20,24},{24,28},{1,5},{5,9},{9,... | collective-permute-start | bytes 393224 | tf_op jit(solution)/shard_map/ppermute | solution.py:13
  13.7 84.6 %collective-permute-start.1 = (bf16[16,32,128]{2,0,1:T(8,128)(2,1)}, bf16[16,32,128]{2,0,1:T(8,128)(2,1)}, u32[]{:S(2)}, u32[]{:S(2)}) collective-permute-start(bf16[16,32,128]{2,0,1:T(8,128)(2,1)} %copy_bitcast_fusion.1), channel_id=1, source_target_pairs={{4,0},{8,4},{12,8},{16,12},{20,16},{24,20},{28,24},{5,1},{9,5},{13... | collective-permute-start | bytes 393224 | tf_op jit(solution)/shard_map/ppermute | solution.py:13
  15.0 84.9 %collective-permute-start.2 = (bf16[16,32,128]{2,0,1:T(8,128)(2,1)}, bf16[16,32,128]{2,0,1:T(8,128)(2,1)}, u32[]{:S(2)}, u32[]{:S(2)}) collective-permute-start(bf16[16,32,128]{2,0,1:T(8,128)(2,1)} %copy_bitcast_fusion.1), channel_id=1, source_target_pairs={{0,8},{4,12},{8,16},{12,20},{16,24},{20,28},{1,9},{5,13},{9,17},{1... | collective-permute-start | bytes 393224 | tf_op jit(solution)/shard_map/ppermute | solution.py:13
  20.5 81.0 %collective-permute-start.3 = (bf16[16,32,128]{2,0,1:T(8,128)(2,1)}, bf16[16,32,128]{2,0,1:T(8,128)(2,1)}, u32[]{:S(2)}, u32[]{:S(2)}) collective-permute-start(bf16[16,32,128]{2,0,1:T(8,128)(2,1)} %copy_bitcast_fusion.1), channel_id=1, source_target_pairs={{8,0},{12,4},{16,8},{20,12},{24,16},{28,20},{9,1},{13,5},{17,9},{2... | collective-permute-start | bytes 393224 | tf_op jit(solution)/shard_map/ppermute | solution.py:13
  21.8 81.2 %collective-permute-start.4 = (bf16[16,32,128]{2,0,1:T(8,128)(2,1)}, bf16[16,32,128]{2,0,1:T(8,128)(2,1)}, u32[]{:S(2)}, u32[]{:S(2)}) collective-permute-start(bf16[16,32,128]{2,0,1:T(8,128)(2,1)} %copy_bitcast_fusion.1), channel_id=1, source_target_pairs={{0,16},{4,20},{8,24},{12,28},{1,17},{5,21},{9,25},{13,29},{2,18},{... | collective-permute-start | bytes 393224 | tf_op jit(solution)/shard_map/ppermute | solution.py:13
  30.1 6.2 %copy-start.17 = (s32[32,2]{0,1:T(2,128)S(1)}, s32[32,2]{0,1:T(2,128)}, u32[]{:S(2)}) copy-start(s32[32,2]{0,1:T(2,128)} %param.15) | copy-start | bytes 772
  30.1 11.3 %copy-start.14 = (s32[32,8]{0,1:T(8,128)S(1)}, s32[32,8]{0,1:T(8,128)}, u32[]{:S(2)}) copy-start(s32[32,8]{0,1:T(8,128)} %param.17) | copy-start | bytes 3076
  41.4 0.6 copy-start.11
  43.4 1.0 copy-start.10
  44.4 37.9 %copy-start.9 = (f32[16,32,32]{2,1,0:T(8,128)S(1)}, f32[16,32,32]{2,1,0:T(8,128)}, u32[]{:S(2)}) copy-start(f32[16,32,32]{2,1,0:T(8,128)} %param.20) | copy-start | bytes 196612
  44.4 38.1 %copy-start.7 = (f32[16,3,32,32]{3,2,1,0:T(8,128)S(1)}, f32[16,3,32,32]{3,2,1,0:T(8,128)}, u32[]{:S(2)}) copy-start(f32[16,3,32,32]{3,2,1,0:T(8,128)} %param.21) | copy-start | bytes 589828
  44.7 43.3 %copy-start.12 = (s32[4,2,32]{2,1,0:T(2,128)S(1)}, s32[4,2,32]{2,1,0:T(2,128)}, u32[]{:S(2)}) copy-start(s32[4,2,32]{2,1,0:T(2,128)} %copy-done.11) | copy-start | bytes 3076
  44.7 43.9 %copy-start.8 = (f32[1,2,32,32]{3,2,1,0:T(8,128)S(1)}, f32[1,2,32,32]{3,2,1,0:T(8,128)}, u32[]{:S(2)}) copy-start(f32[1,2,32,32]{3,2,1,0:T(8,128)} %copy.104) | copy-start | bytes 24580
  44.7 44.0 %copy-start.6 = (f32[1,4,32,32]{3,2,1,0:T(8,128)S(1)}, f32[1,4,32,32]{3,2,1,0:T(8,128)}, u32[]{:S(2)}) copy-start(f32[1,4,32,32]{3,2,1,0:T(8,128)} %copy.103) | copy-start | bytes 49156
  45.3 43.7 %copy-start.5 = (f32[1,8,32,32]{3,2,1,0:T(8,128)S(1)}, f32[1,8,32,32]{3,2,1,0:T(8,128)}, u32[]{:S(2)}) copy-start(f32[1,8,32,32]{3,2,1,0:T(8,128)} %copy.102) | copy-start | bytes 98308
  45.3 44.0 %copy-start.3 = (f32[1,16,32,32]{3,2,1,0:T(8,128)S(1)}, f32[1,16,32,32]{3,2,1,0:T(8,128)}, u32[]{:S(2)}) copy-start(f32[1,16,32,32]{3,2,1,0:T(8,128)} %copy.101) | copy-start | bytes 196612
  46.7 43.2 %copy-start.2 = (f32[32,8,32,32]{3,2,1,0:T(8,128)S(1)}, f32[32,8,32,32]{3,2,1,0:T(8,128)}, u32[]{:S(2)}) copy-start(f32[32,8,32,32]{3,2,1,0:T(8,128)} %param.18) | copy-start | bytes 3145732
  46.7 43.2 %copy-start.15 = (pred[32,8]{1,0:T(8,128)(4,1)S(1)}, pred[32,8]{1,0:T(8,128)(4,1)}, u32[]{:S(2)}) copy-start(pred[32,8]{1,0:T(8,128)(4,1)} %copy.94) | copy-start | bytes 772
  89.9 6.3 %copy-start.13 = (s32[32,8]{0,1:T(8,128)S(1)}, s32[32,8]{0,1:T(8,128)}, u32[]{:S(2)}) copy-start(s32[32,8]{0,1:T(8,128)} %get-tuple-element.19) | copy-start | bytes 3076
  89.9 6.4 %copy-start.16 = (pred[32,8]{0,1:T(8,128)(4,1)S(1)}, pred[32,8]{0,1:T(8,128)(4,1)}, u32[]{:S(2)}) copy-start(pred[32,8]{0,1:T(8,128)(4,1)} %compare_and_fusion.1) | copy-start | bytes 772
  89.9 15.1 %copy-start.23 = (pred[4]{0:T(512)(128)(4,1)S(1)}, pred[4]{0:T(512)(128)(4,1)}, u32[]{:S(2)}) copy-start(pred[4]{0:T(512)(128)(4,1)} %compare_and_fusion.7) | copy-start | bytes 16
  89.9 15.2 %copy-start.22 = (pred[4]{0:T(512)(128)(4,1)S(1)}, pred[4]{0:T(512)(128)(4,1)}, u32[]{:S(2)}) copy-start(pred[4]{0:T(512)(128)(4,1)} %compare_and_fusion.6) | copy-start | bytes 16
  93.8 11.4 %copy-start.21 = (pred[4]{0:T(512)(128)(4,1)S(1)}, pred[4]{0:T(512)(128)(4,1)}, u32[]{:S(2)}) copy-start(pred[4]{0:T(512)(128)(4,1)} %compare_and_fusion.5) | copy-start | bytes 16
  93.8 11.5 %copy-start.20 = (pred[4]{0:T(512)(128)(4,1)S(1)}, pred[4]{0:T(512)(128)(4,1)}, u32[]{:S(2)}) copy-start(pred[4]{0:T(512)(128)(4,1)} %compare_and_fusion.4) | copy-start | bytes 16
  93.8 11.6 %copy-start.19 = (pred[4]{0:T(512)(128)(4,1)S(1)}, pred[4]{0:T(512)(128)(4,1)}, u32[]{:S(2)}) copy-start(pred[4]{0:T(512)(128)(4,1)} %compare_and_fusion.3) | copy-start | bytes 16
  93.8 11.7 %copy-start.18 = (pred[4]{0:T(512)(128)(4,1)S(1)}, pred[4]{0:T(512)(128)(4,1)}, u32[]{:S(2)}) copy-start(pred[4]{0:T(512)(128)(4,1)} %compare_and_fusion.2) | copy-start | bytes 16
  94.8 9.6 %collective-permute-start.5 = (bf16[16,32,128]{2,0,1:T(8,128)(2,1)}, bf16[16,32,128]{2,0,1:T(8,128)(2,1)S(1)}, u32[]{:S(2)}, u32[]{:S(2)}) collective-permute-start(bf16[16,32,128]{2,0,1:T(8,128)(2,1)} %copy_bitcast_fusion.1), channel_id=1, source_target_pairs={{16,0},{20,4},{24,8},{28,12},{17,1},{21,5},{25,9},{29,13},{18,2},{... | collective-permute-start | bytes 393224 | tf_op jit(solution)/shard_map/ppermute | solution.py:13
Sparse Core Ops, SparseCore 0:
  8.9 60.9 all-gather.2
where the time goes:
time: 120 us; the launch traced here: 119 us
  blocking collectives  35.6 us (30%)
  local copies, waits for them, and re-layouts  21.9 us (18%)
  starting transfers between devices  20.5 us (17%)
  matrix products  19.2 us (16%)
  between operations  14.1 us (12%)
  other arithmetic  7.4 us (6%)
    all_gather x1, blocking collectives, local(): roots = lax.all_gather(root_coef[None], 'leaf', axis=0, tiled=True)  30.5 us
    ppermute x6, starting transfers between devices, shifted(): lax.ppermute(value, axis, [(source, source + steps) for source in range(f...  20.5 us
    gather x6, local copies, waits for them, and re-layouts, local(): chosen = jnp.take(neighbour_panels, jnp.maximum(sent_leaf, 0), axis=1)  8.24 us
    unnamed x54, local copies, waits for them, and re-layouts  6.54 us
    dot_general x6, matrix products, lift_pairs(): jnp.einsum('...nrs,...nqr->...nqs', child_maps, child_coef, precision=TOP...  5.4 us
    all_gather x1, blocking collectives, local(): piece_sources = lax.all_gather(near_src, 'rhs', axis=1, tiled=True)  5.06 us
    dot_general x1, matrix products, local(): jnp.einsum('tkij,qtkj->qti', piece_blocks, picked, preferred_element_type...  4.71 us
    dot_general x12, matrix products, apply_maps(): jnp.einsum('...nrs,...nqs->...nqr', node_maps, coef_rows, precision=TOP_P...  4.12 us
  transfers between devices with their start and end apart: 7, of which 0 were waited for; matrix products, arithmetic and copies ran while one was open for 35% of the time, Pallas kernels for 0%

commit v1 on v0

v1 whole, which is shorter than its diff:
```python
import functools

import jax
import jax.numpy as jnp
from jax import lax
from jax.experimental import pallas as pl
from jax.experimental.pallas import tpu as pltpu
from jax.sharding import Mesh
from jax.sharding import PartitionSpec as P

FACE_SIGNS = ((1, 0), (-1, 0), (1, 1), (-1, 1), (1, 2), (-1, 2))
F32 = jnp.float32
BF16 = jnp.bfloat16
LANES = 128
VMEM = pl.BlockSpec(memory_space=pltpu.VMEM)
SMEM = pl.BlockSpec(memory_space=pltpu.SMEM)


def cube_side(device_count):
    return max((edge_len for edge_len in range(1, 65) if edge_len**3 <= device_count))


def face_offsets(device_count):
    side_len = cube_side(device_count)
    return [face_sign * side_len**axis_pos for face_sign, axis_pos in FACE_SIGNS]


def halves(value):
    high = value.astype(BF16)
    return high, (value - high.astype(F32)).astype(BF16)


def dot_nn(left, right):
    return lax.dot_general(left, right, (((1,), (0,)), ((), ())), preferred_element_type=F32)


def dot_nt(left, right):
    return lax.dot_general(left, right, (((1,), (1,)), ((), ())), preferred_element_type=F32)


def split_dot(dot, rows, right_high, right_low):
    count = rows.shape[0]
    high, low = halves(rows)
    both = jnp.concatenate([high, low], axis=0)
    out = dot(both, right_high) + dot(both, right_low)
    return out[:count] + out[count:]


def spread_bases(block, group):
    rank, lanes = block.shape
    width = lanes // group
    zero = jnp.zeros((rank, width), block.dtype)
    rows = []
    for slot in range(group):
        pieces = [zero] * group
        pieces[slot] = block[:, slot * width : (slot + 1) * width]
        rows.append(jnp.concatenate(pieces, axis=1))
    return jnp.concatenate(rows, axis=0)


def level_tiles(leaf_count, group):
    tiles = {}
    level = 1
    while level < leaf_count:
        children = 2 * level
        span = max(group, min(children, 2 * group))
        tiles[level] = [(children + first, span) for first in range(0, children, span)]
        level = children
    return tiles


def tile_mask(first, span, level, rank, group):
    row = lax.broadcasted_iota(jnp.int32, (span * rank, group * rank), 0)
    lane = lax.broadcasted_iota(jnp.int32, (span * rank, group * rank), 1)
    child = row // rank
    return (child // 2 == lane // rank) & (child + first < 4 * level)


def up_kernel(
    offsets, far_groups, where_ref, send_ref, dens_ref, bases_ref, maps_ref,
    coef_ref, high_ref, low_ref, out_ref, spread_ref,
):
    columns, points = dens_ref.shape
    rank = bases_ref.shape[0]
    group = LANES // rank
    node_count = maps_ref.shape[2]
    leaf_count = node_count // 2
    width = points // leaf_count
    device = where_ref[0]
    device_count = out_ref.shape[0] // far_groups
    cap = send_ref.shape[1]
    out_ref[...] = jnp.zeros_like(out_ref)
    for direction, offset in enumerate(offsets):
        target = device + offset

        @pl.when((target >= 0) & (target < device_count))
        def _():
            for place in range(cap):
                leaf = jnp.maximum(send_ref[direction, place, device], 0)
                panel = dens_ref[:, pl.ds(pl.multiple_of(leaf * width, LANES), width)]
                for copy in range(far_groups):
                    out_ref[target * far_groups + copy, place * columns : (place + 1) * columns, :] = panel
    step = group * width
    coefs = []
    for first in range(0, points, step):
        high, low = halves(bases_ref[:, first : first + step])
        dens = dens_ref[:, first : first + step]
        coefs.append(
            dot_nt(dens, spread_bases(high, group)) + dot_nt(dens, spread_bases(low, group))
        )
    coef = jnp.concatenate(coefs, axis=1)
    coef_ref[...] = coef
    for row in range(rank):
        slab = jnp.concatenate([maps_ref[row]] * group, axis=0)
        spread_ref[pl.ds(row, node_count, stride=rank), :] = slab.T
    level = leaf_count // 2
    tiles = level_tiles(leaf_count, group)
    while level >= 1:
        parents = []
        for index, (first, span) in enumerate(tiles[level]):
            rows = slice(first * rank, (first + span) * rank)
            masked = jnp.where(tile_mask(first, span, level, rank, group), spread_ref[rows, :], 0.0)
            high, low = halves(masked)
            place = first - 2 * level
            if level > 1:
                high_ref[rows, :] = high
                low_ref[rows, :] = low
            else:
                high_ref[0 : span * rank, :] = high
                low_ref[0 : span * rank, :] = low
            lanes = slice(place * rank, (place + span) * rank)
            parents.append(split_dot(dot_nn, coef[:, lanes], high, low))
        coef = jnp.concatenate(parents, axis=1) if len(parents) > 1 else parents[0]
        level //= 2
    high = coef.astype(BF16).astype(F32)
    rest = coef - high
    middle = rest.astype(BF16).astype(F32)
    last = (rest - middle).astype(BF16).astype(F32)
    packed = high + pltpu.roll(middle, rank, 1) + pltpu.roll(last, 2 * rank, 1)
    packed = packed.astype(BF16)
    for index in range(out_ref.shape[0]):
        out_ref[index, cap * columns : (cap + 1) * columns, :] = packed


def near_kernel(
    offsets, far_groups, share, where_ref, *refs,
):
    source_refs = refs[:share]
    dens_refs = refs[share : share + far_groups]
    got_ref = refs[share + far_groups]
    block_refs = refs[share + far_groups + 1 : 2 * share + far_groups + 1]
    out_refs = refs[2 * share + far_groups + 1 : -1]
    buffer_ref = refs[-1]
    device, own = where_ref[0], where_ref[1]
    columns, points = dens_refs[0].shape
    leaf_count, near_count, width, _ = block_refs[0].shape
    device_count = got_ref.shape[0] // far_groups
    cap = got_ref.shape[1] // columns - 1
    for part in range(far_groups):
        rows = slice(part * columns, (part + 1) * columns)
        for leaf in range(leaf_count):
            buffer_ref[leaf, rows, :] = dens_refs[part][:, leaf * width : (leaf + 1) * width]
        owner = lax.rem(own + part, far_groups)
        for direction, offset in enumerate(offsets):
            sender = jnp.clip(device - offset, 0, device_count - 1) * far_groups + owner
            for place in range(cap):
                buffer_ref[leaf_count + direction * cap + place, rows, :] = got_ref[
                    sender, place * columns : (place + 1) * columns, :
                ]
    for leaf in range(leaf_count):
        total = None
        for source_ref, block_ref in zip(source_refs, block_refs):
            for block in range(near_count):
                term = dot_nt(buffer_ref[source_ref[block, leaf]], block_ref[leaf, block])
                total = term if total is None else total + term
        for part, out_ref in enumerate(out_refs):
            out_ref[:, leaf * width : (leaf + 1) * width] = total[
                part * columns : (part + 1) * columns
            ]


def far_kernel(
    far_groups, where_ref, far_ref, near_ref, coef_ref, bases_ref, coupling_ref, high_ref, low_ref,
    upper_ref, cross_ref, got_ref, out_ref, turned_ref, local_ref, tree_ref,
):
    device, own = where_ref[0], where_ref[1]
    columns, points = near_ref.shape
    rank = bases_ref.shape[0]
    group = LANES // rank
    leaf_count, far_count = coupling_ref.shape[:2]
    device_count = got_ref.shape[0] // far_groups
    cap = got_ref.shape[1] // columns - 1
    high, low = halves(coef_ref[...])
    both = jnp.concatenate([high.astype(F32), low.astype(F32)], axis=0)
    for first in range(0, leaf_count * rank, LANES):
        turned_ref[first : first + LANES, :] = both[:, first : first + LANES].T.astype(BF16)
    for leaf in range(leaf_count):
        maps = jnp.concatenate([coupling_ref[leaf, j] for j in range(far_count)], axis=1)
        maps = jnp.concatenate(halves(maps), axis=0)
        picked = jnp.concatenate(
            [
                turned_ref[pl.ds(pl.multiple_of(far_ref[j, leaf] * rank, rank), rank), :]
                for j in range(far_count)
            ],
            axis=0,
        )
        out = dot_nn(maps, picked)
        local_ref[leaf * rank : (leaf + 1) * rank, :] = out[:rank] + out[rank:]
    lane = lax.broadcasted_iota(jnp.int32, (LANES, rank), 0)
    column = lax.broadcasted_iota(jnp.int32, (LANES, rank), 1)
    gather = jnp.where((lane % rank == column) & (lane < 3 * rank), 1.0, 0.0).astype(BF16)
    for index in range(device_count):
        piece = got_ref[index * far_groups + own, cap * columns : (cap + 1) * columns, :]
        tree_ref[device_count + index] = dot_nn(piece, gather)
    level = device_count // 2
    while level >= 4:
        for node in range(level, 2 * level):
            total = None
            for child in (2 * node, 2 * node + 1):
                term = split_dot(dot_nn, tree_ref[child], *halves(upper_ref[child]))
                total = term if total is None else total + term
            tree_ref[node] = total
        level //= 2
    field = None
    level = 4
    while level <= device_count:
        place = device // (device_count // level)
        node = level + place
        third = jnp.where(place % 2 == 0, place + 3, place - 3)
        total = None
        for slot, other in enumerate((place - 2, place + 2, third)):
            inside = (other >= 0) & (other < level)
            value = tree_ref[level + jnp.clip(other, 0, level - 1)]
            value = jnp.where(inside, value, 0.0)
            term = split_dot(dot_nt, value, *halves(cross_ref[node, slot]))
            total = term if total is None else total + term
        if field is not None:
            total = total + split_dot(dot_nt, field, *halves(upper_ref[node]))
        field = total
        level *= 2
    field = jnp.concatenate([field, jnp.zeros((columns, LANES - rank), F32)], axis=1)
    tiles = level_tiles(leaf_count, group)
    level = 1
    while level < leaf_count:
        children = []
        for index, (first, span) in enumerate(tiles[level]):
            start = first * rank if level > 1 else 0
            rows = slice(start, start + span * rank)
            lanes = slice(index * LANES, (index + 1) * LANES)
            children.append(split_dot(dot_nt, field[:, lanes], high_ref[rows, :], low_ref[rows, :]))
        field = jnp.concatenate(children, axis=1) if len(children) > 1 else children[0]
        level *= 2
    width = points // leaf_count
    step = group * width
    for index in range(leaf_count // group):
        lanes = slice(index * LANES, (index + 1) * LANES)
        turned = local_ref[lanes, :].T
        rows = field[:, lanes] + turned[:columns] + turned[columns:]
        spots = slice(index * step, (index + 1) * step)
        high, low = halves(bases_ref[:, spots])
        out_ref[:, spots] = near_ref[:, spots] + split_dot(
            dot_nn, rows, spread_bases(high, group), spread_bases(low, group)
        )


def local(
    densities,
    bases,
    near_blocks,
    near_src,
    send_leaf,
    far_src,
    leaf_coupling,
    local_transfer,
    upper_transfer,
    up_coupling,
):
    leaf_devices = lax.axis_size("leaf")
    far_groups = lax.axis_size("far")
    share = lax.axis_size("mate")
    offsets = face_offsets(leaf_devices)
    columns, points = densities.shape
    leaf_count, _, width, _ = near_blocks.shape
    rank = bases.shape[0]
    cap = send_leaf.shape[2]
    node_count = local_transfer.shape[1]
    place = jnp.stack([lax.axis_index("leaf"), lax.axis_index("far")]).astype(jnp.int32)
    params = pltpu.CompilerParams(vmem_limit_bytes=40 * 2**20)

    def rotated(value, axis, shift):
        count = lax.axis_size(axis)
        return lax.ppermute(value, axis, [(i, (i - shift) % count) for i in range(count)])

    sources = near_src.T
    panels = [densities] + [rotated(densities, "far", part) for part in range(1, far_groups)]
    all_sources = [sources] + [rotated(sources, "mate", part) for part in range(1, share)]
    all_blocks = [near_blocks] + [rotated(near_blocks, "mate", part) for part in range(1, share)]

    chunk = (cap + 1) * columns
    coef, high, low, outgoing = pl.pallas_call(
        functools.partial(up_kernel, offsets, far_groups),
        out_shape=[
            jax.ShapeDtypeStruct((columns, leaf_count * rank), F32),
            jax.ShapeDtypeStruct((node_count * rank, LANES), BF16),
            jax.ShapeDtypeStruct((node_count * rank, LANES), BF16),
            jax.ShapeDtypeStruct((leaf_devices * far_groups, chunk, LANES), BF16),
        ],
        in_specs=[SMEM, SMEM, VMEM, VMEM, VMEM],
        out_specs=[VMEM] * 4,
        scratch_shapes=[pltpu.VMEM((node_count * rank, LANES), F32)],
        compiler_params=params,
        name="up",
    )(place, send_leaf.transpose(1, 2, 0), densities, bases, local_transfer[0].transpose(1, 2, 0))
    arrived = lax.all_to_all(outgoing, ("leaf", "far"), 0, 0, tiled=True)

    slots = leaf_count + len(offsets) * cap
    partials = pl.pallas_call(
        functools.partial(near_kernel, offsets, far_groups, share),
        out_shape=[jax.ShapeDtypeStruct((columns, points), F32)] * far_groups,
        in_specs=[SMEM] * (1 + share) + [VMEM] * (far_groups + 1 + share),
        out_specs=[VMEM] * far_groups,
        scratch_shapes=[pltpu.VMEM((slots, far_groups * columns, width), BF16)],
        compiler_params=params,
        name="near",
    )(place, *all_sources, *panels, arrived, *all_blocks)
    received = [rotated(partials[part], "far", -part) for part in range(1, far_groups)]
    total = pl.pallas_call(
        functools.partial(far_kernel, far_groups),
        out_shape=jax.ShapeDtypeStruct((columns, points), F32),
        in_specs=[SMEM] * 2 + [VMEM] * 9,
        out_specs=VMEM,
        scratch_shapes=[
            pltpu.VMEM((leaf_count * rank, 2 * columns), BF16),
            pltpu.VMEM((leaf_count * rank, 2 * columns), F32),
            pltpu.VMEM((2 * leaf_devices, columns, rank), F32),
        ],
        compiler_params=params,
        name="far",
    )(
        place, far_src.T, partials[0], coef, bases, leaf_coupling, high, low, upper_transfer,
        up_coupling, arrived,
    )
    for value in received:
        total = total + value
    return total


def solution(mesh):
    leaf_devices, rhs_devices = mesh.shape["leaf"], mesh.shape["rhs"]
    share = 2 if rhs_devices % 2 == 0 else 1
    split = Mesh(
        mesh.devices.reshape(leaf_devices, rhs_devices // share, share), ("leaf", "far", "mate")
    )
    rhs = ("far", "mate")
    in_specs = (
        P(rhs, "leaf"),
        P(None, "leaf"),
        P("leaf", rhs, None, None),
        P("leaf", rhs),
        P(),
        P("leaf", None),
        P("leaf", None, None, None),
        P("leaf", None, None, None),
        P(),
        P(),
    )
    return jax.shard_map(
        local, mesh=split, in_specs=in_specs, out_specs=P(rhs, "leaf"), check_vma=False
    )
```

time: 120 us -> 44.2 us (0.37)
  blocking collectives: 35.6 us -> 0 us
  matrix products: 19.2 us -> 0 us
  between operations: 14.1 us -> 0.04 us
  Pallas kernels: 0 us -> 9.77 us
  starting transfers between devices: 20.5 us -> 11 us
  local copies, waits for them, and re-layouts: 21.9 us -> 12.6 us
  waiting for transfers between devices: 0.74 us -> 9.41 us
  other arithmetic: 7.4 us -> 0.81 us
    all_gather x2 -> x0, blocking collectives: 35.6 us -> none  [the longest x1 30.5 us: local(): roots = lax.all_gather(root_coef[None], 'leaf', axis=0, tiled=True)]
    dot_general x22 -> x0, matrix products: 19.2 us -> none  [the longest x6 5.4 us: lift_pairs(): jnp.einsum('...nrs,...nqr->...nqs', child_maps, child_coef, precision=TOP...]
    ppermute x6 -> x4, starting transfers between devices: 20.5 us -> 2.97 us  [rotated(): lax.ppermute(value, axis, [(i, (i - shift) % count) for i in range(count)])]
    gather x8 -> x0, local copies, waits for them, and re-layouts: 10.1 us -> none  [the longest x6 8.24 us: local(): chosen = jnp.take(neighbour_panels, jnp.maximum(sent_leaf, 0), axis=1)]
    pallas_call x0 -> x3, Pallas kernels: none -> 9.77 us  [the longest x1 3.51 us: local(): pl.pallas_call(functools.partial(far_kernel, far_groups), out_shape=jax.S...]
    all_to_all x0 -> x1, starting transfers between devices: none -> 8 us  [local(): arrived = lax.all_to_all(outgoing, ('leaf', 'far'), 0, 0, tiled=True)]
    unnamed x54 -> x32, local copies, waits for them, and re-layouts: 6.54 us -> 12.6 us
    ppermute x6 -> x4, waiting for transfers between devices: 0.02 us -> 5.78 us  [rotated(): lax.ppermute(value, axis, [(i, (i - shift) % count) for i in range(count)])]
  transfers between devices with their start and end apart: 7 -> 5, of which waited for: 0 -> 3; matrix products, arithmetic and copies ran while one was open for 35% -> 0% of each run, Pallas kernels for 0% -> 16%
where the time goes in v1:
time: 44.2 us; the launch traced here: 43.6 us
  local copies, waits for them, and re-layouts  12.6 us (29%)
  starting transfers between devices  11 us (25%)
  Pallas kernels  9.77 us (22%)
  waiting for transfers between devices  9.41 us (21%)
  other arithmetic  0.81 us (2%)
    unnamed x32, local copies, waits for them, and re-layouts  12.6 us
    all_to_all x1, starting transfers between devices, local(): arrived = lax.all_to_all(outgoing, ('leaf', 'far'), 0, 0, tiled=True)  8 us
    ppermute x4, waiting for transfers between devices, rotated(): lax.ppermute(value, axis, [(i, (i - shift) % count) for i in range(count)])  5.78 us
    all_to_all x1, waiting for transfers between devices, local(): arrived = lax.all_to_all(outgoing, ('leaf', 'far'), 0, 0, tiled=True)  3.62 us
    pallas_call x1, Pallas kernels, local(): pl.pallas_call(functools.partial(far_kernel, far_groups), out_shape=jax.S...  3.51 us
    pallas_call x1, Pallas kernels, local(): pl.pallas_call(functools.partial(up_kernel, offsets, far_groups), out_sha...  3.37 us
    ppermute x4, starting transfers between devices, rotated(): lax.ppermute(value, axis, [(i, (i - shift) % count) for i in range(count)])  2.97 us
    pallas_call x1, Pallas kernels, local(): pl.pallas_call(functools.partial(near_kernel, offsets, far_groups, share)...  2.88 us
  transfers between devices with their start and end apart: 5, of which 3 were waited for; matrix products, arithmetic and copies ran while one was open for 0% of the time, Pallas kernels for 16%

profile of v1, /device:TPU:0, one launch (start us, length us, event | category | flops | bytes accessed | tf_op | source)
XLA Modules:
  0.0 43.6 jit_solution(12512181983468938564)
XLA Ops:
  0.0 0.5 %collective-permute-start.2 = (bf16[32,2,128,128]{3,2,1,0:T(8,128)(2,1)}, bf16[32,2,128,128]{3,2,1,0:T(8,128)(2,1)S(1)}, u32[]{:S(2)}, u32[]{:S(2)}) collective-permute-start(bf16[32,2,128,128]{3,2,1,0:T(8,128)(2,1)} %refs_5_.1), channel_id=1, source_target_pairs={{0,1},{1,0},{2,3},{3,2},{4,5},{5,4},{6,7},{7,6},{8,9},{9,8},{10,11... | collective-permute-start | bytes 6291464 | tf_op jit(solution)/shard_map/ppermute | solution.py:292
  0.5 0.1 pad_add_fusion.where_ref
  0.5 0.0 copy-start.1
  0.5 1.0 %copy-done.1 = f32[32,4096]{1,0:T(8,128)S(1)} copy-done((f32[32,4096]{1,0:T(8,128)S(1)}, f32[32,4096]{1,0:T(8,128)}, u32[]{:S(2)}) %copy-start.1) | copy-done | bytes 524312
  1.6 0.9 %copy-done.7 = bf16[16,4096]{1,0:T(8,128)(2,1)S(1)} copy-done((bf16[16,4096]{1,0:T(8,128)(2,1)S(1)}, bf16[16,4096]{1,0:T(8,128)(2,1)}, u32[]{:S(2)}) %copy-start.7) | copy-done | bytes 131096
  2.5 1.0 %copy-done.9 = f32[1,64,32,32]{1,3,2,0:T(8,128)S(1)} copy-done((f32[1,64,32,32]{1,3,2,0:T(8,128)S(1)}, f32[1,64,32,32]{1,3,2,0:T(8,128)}, u32[]{:S(2)}) %copy-start.9) | copy-done | bytes 262168
  3.5 0.7 %copy-done.13 = s32[8,6,4]{0,2,1:T(4,128)S(1)} copy-done((s32[8,6,4]{0,2,1:T(4,128)S(1)}, s32[8,6,4]{0,2,1:T(4,128)}, u32[]{:S(2)}) %copy-start.13) | copy-done | bytes 792
  4.2 3.4 %up.1 = (f32[16,1024]{1,0:T(8,128)S(1)}, bf16[2048,128]{1,0:T(8,128)(2,1)S(1)}, bf16[2048,128]{1,0:T(8,128)(2,1)S(1)}, bf16[16,80,128]{2,1,0:T(8,128)(2,1)}) custom-call(s32[2]{0:T(128)S(1)} %pad_add_fusion.where_ref, s32[6,4,8]{2,1,0:T(4,128)S(1)} %bitcast.9, bf16[16,4096]{1,0:T(8,128)(2,1)S(1)} %copy-done.7, f32[32,4096]{1,0:T(8,128)S(1)} %copy-done.1, ...), custom_call_target="tpu_custom_call" | custom-call | tf_op jit(solution)/shard_map/up/pallas_call | solution.py:300
  7.6 0.8 %copy-done.5 = bf16[2048,128]{1,0:T(8,128)(2,1)} copy-done((bf16[2048,128]{1,0:T(8,128)(2,1)}, bf16[2048,128]{1,0:T(8,128)(2,1)S(1)}, u32[]{:S(2)}) %copy-start.5) | copy-done | bytes 524312
  8.4 8.0 %all-to-all-start = ((bf16[16,80,128]{2,1,0:T(8,128)(2,1)}), bf16[16,80,128]{2,1,0:T(8,128)(2,1)S(1)}, u32[]{:S(2)}, u32[]{:S(2)}) async-start(bf16[16,80,128]{2,1,0:T(8,128)(2,1)} %get-tuple-element.11), calls=%async_computation | async-start | bytes 655360 | tf_op jit(solution)/shard_map/all_to_all | solution.py:314
  16.4 1.9 %collective-permute-start.1 = (bf16[16,4096]{1,0:T(8,128)(2,1)}, bf16[16,4096]{1,0:T(8,128)(2,1)S(1)}, u32[]{:S(2)}, u32[]{:S(2)}) collective-permute-start(bf16[16,4096]{1,0:T(8,128)(2,1)} %refs_2_.1), channel_id=1, source_target_pairs={{0,2},{2,0},{1,3},{3,1},{4,6},{6,4},{5,7},{7,5},{8,10},{10,8},{9,1... | collective-permute-start | bytes 393224 | tf_op jit(solution)/shard_map/ppermute | solution.py:292
  18.3 0.0 collective-permute-start
  18.3 1.3 %collective-permute-done.refs_1_ = s32[2,32]{1,0:T(2,128)S(1)} collective-permute-done((s32[2,32]{1,0:T(2,128)}, s32[2,32]{1,0:T(2,128)S(1)}, u32[]{:S(2)}, u32[]{:S(2)}) %collective-permute-start) | collective-permute-done | bytes 288 | tf_op jit(solution)/shard_map/ppermute | solution.py:292
  19.7 4.4 %collective-permute-done.1.refs_3_ = bf16[16,4096]{1,0:T(8,128)(2,1)S(1)} collective-permute-done((bf16[16,4096]{1,0:T(8,128)(2,1)}, bf16[16,4096]{1,0:T(8,128)(2,1)S(1)}, u32[]{:S(2)}, u32[]{:S(2)}) %collective-permute-start.1) | collective-permute-done | bytes 131104 | tf_op jit(solution)/shard_map/ppermute | solution.py:292
  24.1 0.7 %copy-done.11 = bf16[16,4096]{1,0:T(8,128)(2,1)} copy-done((bf16[16,4096]{1,0:T(8,128)(2,1)}, bf16[16,4096]{1,0:T(8,128)(2,1)S(1)}, u32[]{:S(2)}) %copy-start.11) | copy-done | bytes 131096
  24.8 3.6 %all-to-all-done.refs_4_.got_ref = bf16[16,80,128]{2,1,0:T(8,128)(2,1)S(1)} async-done(((bf16[16,80,128]{2,1,0:T(8,128)(2,1)}), bf16[16,80,128]{2,1,0:T(8,128)(2,1)S(1)}, u32[]{:S(2)}, u32[]{:S(2)}) %all-to-all-start) | async-done | bytes 327712 | tf_op jit(solution)/shard_map/all_to_all | solution.py:314
  28.4 0.0 collective-permute-done.2.refs_6_
  28.4 1.7 %copy-done.3 = bf16[32,2,128,128]{3,2,1,0:T(8,128)(2,1)S(1)} copy-done((bf16[32,2,128,128]{3,2,1,0:T(8,128)(2,1)S(1)}, bf16[32,2,128,128]{3,2,1,0:T(8,128)(2,1)}, u32[]{:S(2)}) %copy-start.3) | copy-done | bytes 2097176
  30.1 1.0 %copy-done.8 = bf16[16,4096]{1,0:T(8,128)(2,1)S(1)} copy-done((bf16[16,4096]{1,0:T(8,128)(2,1)S(1)}, bf16[16,4096]{1,0:T(8,128)(2,1)}, u32[]{:S(2)}) %copy-start.8) | copy-done | bytes 131096
  31.2 0.9 %copy-done.12 = bf16[16,4096]{1,0:T(8,128)(2,1)S(1)} copy-done((bf16[16,4096]{1,0:T(8,128)(2,1)S(1)}, bf16[16,4096]{1,0:T(8,128)(2,1)}, u32[]{:S(2)}) %copy-start.12) | copy-done | bytes 131096
  32.1 0.7 %copy-done.15 = s32[32,2]{0,1:T(2,128)S(1)} copy-done((s32[32,2]{0,1:T(2,128)S(1)}, s32[32,2]{0,1:T(2,128)}, u32[]{:S(2)}) %copy-start.15) | copy-done | bytes 280
  32.8 2.9 %near.1 = (f32[16,4096]{1,0:T(8,128)S(1)}, f32[16,4096]{1,0:T(8,128)S(1)}) custom-call(s32[2]{0:T(128)S(1)} %pad_add_fusion.where_ref, s32[2,32]{1,0:T(2,128)S(1)} %bitcast.12, s32[2,32]{1,0:T(2,128)S(1)} %collective-permute-done.refs_1_, bf16[16,4096]{1,0:T(8,128)(2,1)S(1)} %copy-done.8, bf16[16,4096]{1,0:T(8,128)(2,1)S(1)} %copy-done.12, ...), custom_call_target="tpu_custom_call" | custom-call | tf_op jit(solution)/shard_map/near/pallas_call | solution.py:317
  35.7 0.6 %collective-permute-start.3 = (f32[16,4096]{1,0:T(8,128)S(1)}, f32[16,4096]{1,0:T(8,128)S(1)}, u32[]{:S(2)}, u32[]{:S(2)}) collective-permute-start(f32[16,4096]{1,0:T(8,128)S(1)} %get-tuple-element.16), channel_id=1, source_target_pairs={{0,2},{2,0},{1,3},{3,1},{4,6},{6,4},{5,7},{7,5},{8,10},{10,8},{9,1... | collective-permute-start | bytes 786440 | tf_op jit(solution)/shard_map/ppermute | solution.py:292
  36.3 0.0 copy-done.14
  36.3 0.0 copy-done.2
  36.3 0.0 copy-done
  36.3 1.1 %copy-done.4 = f32[16,3,32,32]{3,2,1,0:T(8,128)S(1)} copy-done((f32[16,3,32,32]{3,2,1,0:T(8,128)S(1)}, f32[16,3,32,32]{3,2,1,0:T(8,128)}, u32[]{:S(2)}) %copy-start.4) | copy-done | bytes 196632
  37.4 1.0 %copy-done.6 = bf16[2048,128]{1,0:T(8,128)(2,1)S(1)} copy-done((bf16[2048,128]{1,0:T(8,128)(2,1)S(1)}, bf16[2048,128]{1,0:T(8,128)(2,1)}, u32[]{:S(2)}) %copy-start.6) | copy-done | bytes 524312
  38.4 0.9 %copy-done.10 = f32[16,32,32]{2,1,0:T(8,128)S(1)} copy-done((f32[16,32,32]{2,1,0:T(8,128)S(1)}, f32[16,32,32]{2,1,0:T(8,128)}, u32[]{:S(2)}) %copy-start.10) | copy-done | bytes 65560
  39.4 3.5 %far.1 = f32[16,4096]{1,0:T(8,128)S(1)} custom-call(s32[2]{0:T(128)S(1)} %pad_add_fusion.where_ref, s32[8,32]{1,0:T(8,128)S(1)} %bitcast.10, f32[16,4096]{1,0:T(8,128)S(1)} %get-tuple-element.12.near_ref, f32[16,1024]{1,0:T(8,128)S(1)} %get-tuple-element.13.coef_ref, f32[32,4096]{1,0:T(8,128)S(1)} %copy-done.2, f32[32,8,32,32]{3,2,1,0:T(8,128)S(1)} %copy-done, ...), custom_call_target="tpu_custom_call" | custom-call | tf_op jit(solution)/shard_map/far/pallas_call | solution.py:327
  42.9 0.0 collective-permute-done.3
  42.9 0.7 %add.3 = f32[16,4096]{1,0:T(8,128)} add(f32[16,4096]{1,0:T(8,128)S(1)} %far.1, f32[16,4096]{1,0:T(8,128)S(1)} %collective-permute-done.3) | non-fusion elementwise | flops 65536 | bytes 786432 | tf_op jit(solution)/shard_map/add | solution.py:344
  (15 shorter events, 0.0 us)
Async XLA Ops:
  0.0 28.4 %collective-permute-start.2 = (bf16[32,2,128,128]{3,2,1,0:T(8,128)(2,1)}, bf16[32,2,128,128]{3,2,1,0:T(8,128)(2,1)S(1)}, u32[]{:S(2)}, u32[]{:S(2)}) collective-permute-start(bf16[32,2,128,128]{3,2,1,0:T(8,128)(2,1)} %refs_5_.1), channel_id=1, source_target_pairs={{0,1},{1,0},{2,3},{3,2},{4,5},{5,4},{6,7},{7,6},{8,9},{9,8},{10,11... | collective-permute-start | bytes 6291464 | tf_op jit(solution)/shard_map/ppermute | solution.py:292
  0.5 1.0 %copy-start.1 = (f32[32,4096]{1,0:T(8,128)S(1)}, f32[32,4096]{1,0:T(8,128)}, u32[]{:S(2)}) copy-start(f32[32,4096]{1,0:T(8,128)} %bases_ref.3) | copy-start | bytes 1572868
  1.6 0.9 %copy-start.7 = (bf16[16,4096]{1,0:T(8,128)(2,1)S(1)}, bf16[16,4096]{1,0:T(8,128)(2,1)}, u32[]{:S(2)}) copy-start(bf16[16,4096]{1,0:T(8,128)(2,1)} %refs_2_.1) | copy-start | bytes 393220
  2.5 1.0 %copy-start.9 = (f32[1,64,32,32]{1,3,2,0:T(8,128)S(1)}, f32[1,64,32,32]{1,3,2,0:T(8,128)}, u32[]{:S(2)}) copy-start(f32[1,64,32,32]{1,3,2,0:T(8,128)} %param.17) | copy-start | bytes 786436
  3.5 0.7 %copy-start.13 = (s32[8,6,4]{0,2,1:T(4,128)S(1)}, s32[8,6,4]{0,2,1:T(4,128)}, u32[]{:S(2)}) copy-start(s32[8,6,4]{0,2,1:T(4,128)} %param.14) | copy-start | bytes 2308
  7.6 0.8 %copy-start.5 = (bf16[2048,128]{1,0:T(8,128)(2,1)}, bf16[2048,128]{1,0:T(8,128)(2,1)S(1)}, u32[]{:S(2)}) copy-start(bf16[2048,128]{1,0:T(8,128)(2,1)S(1)} %get-tuple-element.15.low_ref) | copy-start | bytes 1572868
  8.4 27.9 %copy-start.14 = (s32[32,8]{0,1:T(8,128)S(1)}, s32[32,8]{0,1:T(8,128)}, u32[]{:S(2)}) copy-start(s32[32,8]{0,1:T(8,128)} %param.15) | copy-start | bytes 3076
  8.4 20.0 %all-to-all-start = ((bf16[16,80,128]{2,1,0:T(8,128)(2,1)}), bf16[16,80,128]{2,1,0:T(8,128)(2,1)S(1)}, u32[]{:S(2)}, u32[]{:S(2)}) async-start(bf16[16,80,128]{2,1,0:T(8,128)(2,1)} %get-tuple-element.11), calls=%async_computation | async-start | bytes 655360 | tf_op jit(solution)/shard_map/all_to_all | solution.py:314
  16.4 7.7 %collective-permute-start.1 = (bf16[16,4096]{1,0:T(8,128)(2,1)}, bf16[16,4096]{1,0:T(8,128)(2,1)S(1)}, u32[]{:S(2)}, u32[]{:S(2)}) collective-permute-start(bf16[16,4096]{1,0:T(8,128)(2,1)} %refs_2_.1), channel_id=1, source_target_pairs={{0,2},{2,0},{1,3},{3,1},{4,6},{6,4},{5,7},{7,5},{8,10},{10,8},{9,1... | collective-permute-start | bytes 393224 | tf_op jit(solution)/shard_map/ppermute | solution.py:292
  18.3 17.9 %copy-start.2 = (f32[32,4096]{1,0:T(8,128)S(1)}, f32[32,4096]{1,0:T(8,128)}, u32[]{:S(2)}) copy-start(f32[32,4096]{1,0:T(8,128)} %bases_ref.3) | copy-start | bytes 1572868
  18.3 1.4 %collective-permute-start = (s32[2,32]{1,0:T(2,128)}, s32[2,32]{1,0:T(2,128)S(1)}, u32[]{:S(2)}, u32[]{:S(2)}) collective-permute-start(s32[2,32]{1,0:T(2,128)} %bitcast.11), channel_id=1, source_target_pairs={{0,1},{1,0},{2,3},{3,2},{4,5},{5,4},{6,7},{7,6},{8,9},{9,8},{10,11... | collective-permute-start | bytes 776 | tf_op jit(solution)/shard_map/ppermute | solution.py:292
  24.1 0.7 %copy-start.11 = (bf16[16,4096]{1,0:T(8,128)(2,1)}, bf16[16,4096]{1,0:T(8,128)(2,1)S(1)}, u32[]{:S(2)}) copy-start(bf16[16,4096]{1,0:T(8,128)(2,1)S(1)} %collective-permute-done.1.refs_3_) | copy-start | bytes 393220
  28.4 7.9 %copy-start = (f32[32,8,32,32]{3,2,1,0:T(8,128)S(1)}, f32[32,8,32,32]{3,2,1,0:T(8,128)}, u32[]{:S(2)}) copy-start(f32[32,8,32,32]{3,2,1,0:T(8,128)} %coupling_ref.1) | copy-start | bytes 3145732
  28.4 1.7 %copy-start.3 = (bf16[32,2,128,128]{3,2,1,0:T(8,128)(2,1)S(1)}, bf16[32,2,128,128]{3,2,1,0:T(8,128)(2,1)}, u32[]{:S(2)}) copy-start(bf16[32,2,128,128]{3,2,1,0:T(8,128)(2,1)} %refs_5_.1) | copy-start | bytes 6291460
  30.1 1.0 %copy-start.8 = (bf16[16,4096]{1,0:T(8,128)(2,1)S(1)}, bf16[16,4096]{1,0:T(8,128)(2,1)}, u32[]{:S(2)}) copy-start(bf16[16,4096]{1,0:T(8,128)(2,1)} %refs_2_.1) | copy-start | bytes 393220
  31.2 0.9 %copy-start.12 = (bf16[16,4096]{1,0:T(8,128)(2,1)S(1)}, bf16[16,4096]{1,0:T(8,128)(2,1)}, u32[]{:S(2)}) copy-start(bf16[16,4096]{1,0:T(8,128)(2,1)} %copy-done.11) | copy-start | bytes 393220
  32.1 0.7 %copy-start.15 = (s32[32,2]{0,1:T(2,128)S(1)}, s32[32,2]{0,1:T(2,128)}, u32[]{:S(2)}) copy-start(s32[32,2]{0,1:T(2,128)} %param.13) | copy-start | bytes 772
  35.7 7.2 %collective-permute-start.3 = (f32[16,4096]{1,0:T(8,128)S(1)}, f32[16,4096]{1,0:T(8,128)S(1)}, u32[]{:S(2)}, u32[]{:S(2)}) collective-permute-start(f32[16,4096]{1,0:T(8,128)S(1)} %get-tuple-element.16), channel_id=1, source_target_pairs={{0,2},{2,0},{1,3},{3,1},{4,6},{6,4},{5,7},{7,5},{8,10},{10,8},{9,1... | collective-permute-start | bytes 786440 | tf_op jit(solution)/shard_map/ppermute | solution.py:292
  36.3 1.1 %copy-start.4 = (f32[16,3,32,32]{3,2,1,0:T(8,128)S(1)}, f32[16,3,32,32]{3,2,1,0:T(8,128)}, u32[]{:S(2)}) copy-start(f32[16,3,32,32]{3,2,1,0:T(8,128)} %cross_ref.1) | copy-start | bytes 589828
  37.4 1.0 %copy-start.6 = (bf16[2048,128]{1,0:T(8,128)(2,1)S(1)}, bf16[2048,128]{1,0:T(8,128)(2,1)}, u32[]{:S(2)}) copy-start(bf16[2048,128]{1,0:T(8,128)(2,1)} %copy-done.5) | copy-start | bytes 1572868
  38.4 0.9 %copy-start.10 = (f32[16,32,32]{2,1,0:T(8,128)S(1)}, f32[16,32,32]{2,1,0:T(8,128)}, u32[]{:S(2)}) copy-start(f32[16,32,32]{2,1,0:T(8,128)} %upper_ref.1) | copy-start | bytes 196612
